TPU v7x, 32 devices: a whole 2x2x4 slice. The times are simulated.
32 devices in a mesh: pairs: 2 (over x), src: 16 (over z, y, core).
Axes of the slice: x: 2, y: 2, z: 4, core: 2. Of those that a mesh axis runs over, the one named last changes fastest.
Arguments:
- src_feat: bfloat16 [32768, 256], P(('pairs', 'src')), parts along dimension 0, may hold values from -6 to 6
- tile_feat: bfloat16 [256, 16, 128, 256], P(('pairs', 'src')), parts along dimension 0, may hold values from -6 to 6
- tile_tgt: int32 [256, 16], P(('pairs', 'src')), parts along dimension 0, may hold values from 0 to 127, as said below
- tile_live: int32 [256], P(('pairs', 'src')), parts along dimension 0, may hold values from 1 to 16, as said below
- src_lin: float32 [32768], P(('pairs', 'src')), parts along dimension 0, may hold values from 0 to 1
- tgt_lin: float32 [32768], P(('pairs', 'src')), parts along dimension 0, may hold values from 0 to 1
- src_mass: float32 [32768], P(('pairs', 'src')), parts along dimension 0, may hold values from 0.5 to 2
- tgt_mass: float32 [32768], P(('pairs', 'src')), parts along dimension 0, may hold values from 0.25 to 6
- tgt_count: int32 [256], P(('pairs', 'src')), parts along dimension 0, may hold values from 1 to 128
Outputs:
- src_scale: float32 [32768], P(('pairs', 'src')), parts along dimension 0
- tgt_scale: float32 [32768], P(('pairs', 'src')), parts along dimension 0
There are 2 independent parts, one for each index of `pairs`. A program takes and returns all parts, laid end to end along the dimension named above; each array names one. Nothing has to cross between parts.
Inputs may be any that keep to these rules, and one draw needn't show every extreme that they name: tile_tgt[s, 0] = s; the slots of one source block name distinct target blocks. `tile_live`: every source block has between 1 and 16 live slots.
All inputs are finite; a program needn't handle non-finite values.
Results may differ from a plain program's by a relative error of at most 0.0003.
Values sent between devices are 32-bit elements; how exact they have to be, the bound alone decides.
No kernel may reach another device: no remote copies, remote signals or barrier semaphores. Data moves between devices by JAX's collectives and lax.ppermute only.
A program may use at most 64 MiB of HBM per device.

v0:
```python
import jax
import jax.numpy as jnp
from jax import lax
from jax.sharding import PartitionSpec as P

ITERS = 3


EPS = 0.1
RHO = 1.0
ALPHA = 0.5


def shards(
    src_feat, tile_feat, tile_tgt, tile_live, src_lin, tgt_lin, src_mass, tgt_mass, tgt_count
):
    expo = RHO / (RHO + EPS)
    local_blocks = tgt_count.shape[0]
    slots = tile_feat.shape[1]
    block = tile_feat.shape[2]
    width = tile_feat.shape[3]
    all_blocks = local_blocks * lax.axis_size("src")
    src_rows = src_feat.reshape(local_blocks, block, width)
    src_sq = jnp.sum(jnp.square(src_rows.astype(jnp.float32)), axis=-1)
    tiles_sq = jnp.sum(jnp.square(tile_feat.astype(jnp.float32)), axis=-1)
    valid = (lax.broadcasted_iota(jnp.int32, (local_blocks, block), 1) < tgt_count[:, None]).astype(
        jnp.float32
    )
    bmass_own = tgt_mass.reshape(local_blocks, block) * valid
    live_mask = (
        lax.broadcasted_iota(jnp.int32, (local_blocks, slots), 1) < tile_live[:, None]
    ).astype(jnp.float32)
    amass = src_mass.reshape(local_blocks, block)
    src_part = src_lin.reshape(local_blocks, block)
    sum_source, sum_target = lax.psum((jnp.sum(amass), jnp.sum(bmass_own)), "src")
    target_total = jnp.sqrt(sum_source * sum_target)
    lin_full = lax.all_gather(tgt_lin.reshape(local_blocks, block), "src", axis=0, tiled=True)
    tile_lin = lin_full[tile_tgt]
    onehot = (
        lax.broadcasted_iota(jnp.int32, (all_blocks, local_blocks * slots), 0)
        == tile_tgt.reshape(-1)[None, :]
    ).astype(jnp.float32)
    tgt_own = valid
    src_scale = jnp.zeros((local_blocks, block), jnp.float32)
    for iteration in range(ITERS):
        tile_scale = lax.all_gather(tgt_own, "src", axis=0, tiled=True)[tile_tgt]
        cross = jnp.einsum(
            "sid,skjd->skij", src_rows, tile_feat, preferred_element_type=jnp.float32
        )
        cost = (src_sq[:, None, :, None] + tiles_sq[:, :, None, :] - 2.0 * cross) / width - 2.0
        cost = cost + ALPHA * (src_part[:, None, :, None] + tile_lin[:, :, None, :])
        kernel = jnp.exp(-cost / EPS) * live_mask[:, :, None, None]
        row_sums = jnp.einsum("skij,skj->si", kernel, tile_scale, precision=lax.Precision.HIGHEST)
        src_scale = (amass / row_sums) ** expo
        col_parts = jnp.einsum("skij,si->skj", kernel, src_scale, precision=lax.Precision.HIGHEST)
        dense = jnp.dot(
            onehot, col_parts.reshape(local_blocks * slots, block), precision=lax.Precision.HIGHEST
        )
        col_sums = lax.psum_scatter(dense, "src", scatter_dimension=0, tiled=True)
        present = bmass_own > 0.0
        tgt_own = jnp.where(present, (bmass_own / jnp.where(present, col_sums, 1.0)) ** expo, 0.0)
        mass = lax.psum(jnp.sum(tgt_own * col_sums), "src")
        factor = jnp.sqrt(target_total / mass)
        tgt_own = tgt_own * factor
        src_scale = src_scale * factor
    return (src_scale.reshape(-1), tgt_own.reshape(-1))


def solution(mesh):
    in_specs = (
        P(("pairs", "src"), None),
        P(("pairs", "src"), None, None, None),
        P(("pairs", "src"), None),
        P(("pairs", "src")),
        P(("pairs", "src")),
        P(("pairs", "src")),
        P(("pairs", "src")),
        P(("pairs", "src")),
        P(("pairs", "src")),
    )
    out_specs = (P(("pairs", "src")), P(("pairs", "src")))
    return jax.shard_map(shards, mesh=mesh, in_specs=in_specs, out_specs=out_specs, check_vma=False)
```

profile of v0, /device:TPU:0, one launch (start us, length us, event | category | flops | bytes accessed | tf_op | source)
XLA Modules:
  0.0 510.8 jit_solution(15567185982880113961)
XLA Ops:
  7.2 0.0 copy-start.2
  7.2 0.0 copy-start.6
  7.2 0.0 copy-start.5
  7.2 0.0 copy-start.7
  7.2 0.0 all-reduce.8.cloned.1.call-start
  7.3 0.7 compare_select_fusion
  8.0 0.8 eq.10
  8.8 0.1 reshape.73
  8.8 23.5 %all_gather.12 = f32[128,128]{1,0:T(8,128)S(1)} all-gather(f32[8,128]{1,0:T(8,128)} %bitcast.144), channel_id=1, replica_groups=mesh['pairs'=2,'src'=16] {'src'}, dimensions={0}, use_global_device_ids=true | all-gather | bytes 69632 | tf_op jit(solution)/shard_map/all_gather | solution.py:37
  32.4 5.6 %multiply_reduce_fusion = f32[8,16,128]{2,1,0:T(8,128)S(1)} fusion(bf16[8,16,128,256]{3,2,1,0:T(8,128)(2,1)} %param.10), kind=kLoop, calls=%fused_computation.4 | loop fusion | flops 12566528 | bytes 8454144 | tf_op jit(solution)/shard_map/reduce_sum | solution.py:25
  38.0 0.0 copy-done.2
  38.0 0.2 multiply_reduce_fusion.1
  38.2 0.0 copy-done.6
  38.2 0.1 fusion.18
  38.3 0.0 copy-done.5
  38.3 0.1 fusion.17
  38.4 17.8 %all_gather.13 = f32[128,128]{1,0:T(8,128)S(1)} all-gather(f32[8,128]{1,0:T(8,128)S(1)} %fusion.17), channel_id=1, replica_groups=mesh['pairs'=2,'src'=16] {'src'}, dimensions={0}, use_global_device_ids=true | all-gather | bytes 69632 | tf_op jit(solution)/shard_map/all_gather | solution.py:46
  56.1 0.6 gather_fusion
  56.8 0.6 gather_fusion.1
  57.4 0.0 copy-done.7
  57.4 7.9 %fusion.6 = f32[8,16,128,128]{2,3,1,0:T(8,128)S(1)} fusion(f32[8,16]{1,0:T(8,128)S(1)} %fusion.18, f32[8,16,128]{2,1,0:T(8,128)S(1)} %bitcast.135, f32[8,128]{1,0:T(8,128)S(1)} %bitcast.145, f32[8,16,128]{2,1,0:T(8,128)S(1)} %multiply_reduce_fusion, f32[8,128]{1,0:T(8,128)S(1)} %bitcast.143, bf16[8,16,128,256]{3,2,1,0:T(8,128)(2,1)} %param.10, ...), kind=kOutput, calls=%fused_computation.12 | convolution fusion | flops 1096810496 | bytes 17441280 | tf_op jit(solution)/shard_map/sid,skjd->skij/dot_general | solution.py:47
  65.3 0.0 copy-start
  65.3 0.0 copy-start.4
  65.4 0.0 copy-start.3
  65.4 0.0 copy-start.8
  65.4 4.6 fusion.19
  69.9 0.0 copy-done.4
  70.0 7.1 %fusion.20 = f32[8,1,16,128]{3,1,2,0:T(1,128)S(1)} fusion(f32[8,16,128,128]{2,3,1,0:T(8,128)S(1)} %fusion.6, f32[8,128,1,1]{1,2,3,0:T(1,128)S(1)} %bitcast.139), kind=kOutput, calls=%fused_computation.47 | convolution fusion | flops 25165824 | bytes 8458240 | tf_op jit(solution)/shard_map/skij,si->skj/dot_general | solution.py:55
  77.1 0.0 copy-done
  77.1 0.8 fusion.9
  77.9 0.0 all-reduce.8.cloned.1.call-update
  77.9 0.0 all-reduce.10.cloned.1.call-start
  78.0 0.0 copy-done.3
  78.0 0.7 select_reduce_fusion
  78.6 0.6 reduce_sum.65
  79.2 0.0 copy-done.8
  79.2 0.6 dynamic-slice
  80.6 80.4 %all-reduce.8.cloned.1.call-done = f32[128,128]{1,0:T(8,128)} async-done(((f32[128,128]{1,0:T(8,128)}), f32[128,128]{1,0:T(8,128)}) %all-reduce.8.cloned.1.call-update) | async-done | bytes 65552
  160.9 1.3 multiply_reduce_fusion.4
  162.3 32.4 %all-reduce.3 = (f32[]{:T(128)}, f32[]{:T(128)}, f32[]{:T(128)}) all-reduce(f32[]{:T(128)} %reduce_sum.65, f32[]{:T(128)} %select_reduce_fusion, f32[]{:T(128)} %multiply_reduce_fusion.4), channel_id=1, replica_groups=mesh['pairs'=2,'src'=16] {'src'}, use_global_device_ids=true, to_apply=%region_4.0 | all-reduce | flops 3 | bytes 24 | tf_op jit(solution)/shard_map/psum | solution.py:35
  196.6 0.8 broadcast_multiply_fusion.1
  197.4 17.5 %all_gather.14 = f32[128,128]{1,0:T(8,128)S(1)} all-gather(f32[8,128]{1,0:T(8,128)S(1)} %broadcast_multiply_fusion.1), channel_id=1, replica_groups=mesh['pairs'=2,'src'=16] {'src'}, dimensions={0}, use_global_device_ids=true | all-gather | bytes 69632 | tf_op jit(solution)/shard_map/all_gather | solution.py:46
  214.9 0.6 gather_fusion.2
  215.6 0.0 copy-start.1
  215.6 7.6 %fusion.21 = f32[8,1,128,1]{2,1,3,0:T(1,128)S(1)} fusion(f32[8,16,128,128]{2,3,1,0:T(8,128)} %copy-done, f32[8,16,128,1]{2,3,1,0:T(1,128)S(1)} %bitcast.131), kind=kOutput, calls=%fused_computation.48 | convolution fusion | flops 25165824 | bytes 8458240 | tf_op jit(solution)/shard_map/skij,skj->si/dot_general | solution.py:53
  223.2 0.0 copy-done.1
  223.2 7.1 %fusion.22 = f32[8,1,16,128]{3,1,2,0:T(1,128)S(1)} fusion(f32[8,16,128,128]{2,3,1,0:T(8,128)S(1)} %copy-done.1, f32[8,128,1,1]{1,2,3,0:T(1,128)S(1)} %bitcast.141), kind=kOutput, calls=%fused_computation.49 | convolution fusion | flops 25165824 | bytes 8458240 | tf_op jit(solution)/shard_map/skij,si->skj/dot_general | solution.py:55
  230.3 0.8 fusion.8
  231.1 0.0 all-reduce.10.cloned.1.call-update
  231.2 0.0 all-reduce.12.cloned.1.call-start
  231.2 83.3 %all-reduce.10.cloned.1.call-done = f32[128,128]{1,0:T(8,128)} async-done(((f32[128,128]{1,0:T(8,128)}), f32[128,128]{1,0:T(8,128)}) %all-reduce.10.cloned.1.call-update) | async-done | bytes 65552
  314.5 1.4 multiply_reduce_fusion.3
  315.9 32.4 %psum.38 = f32[]{:T(128)} all-reduce(f32[]{:T(128)} %multiply_reduce_fusion.3), channel_id=1, replica_groups=mesh['pairs'=2,'src'=16] {'src'}, use_global_device_ids=true, to_apply=%region_11.12 | all-reduce | flops 1 | bytes 8 | tf_op jit(solution)/shard_map/psum | solution.py:62
  349.0 0.8 broadcast_multiply_fusion
  349.7 17.6 %all_gather.15 = f32[128,128]{1,0:T(8,128)S(1)} all-gather(f32[8,128]{1,0:T(8,128)S(1)} %broadcast_multiply_fusion), channel_id=1, replica_groups=mesh['pairs'=2,'src'=16] {'src'}, dimensions={0}, use_global_device_ids=true | all-gather | bytes 69632 | tf_op jit(solution)/shard_map/all_gather | solution.py:46
  367.3 0.6 gather_fusion.3
  368.0 6.9 %fusion.23 = f32[8,1,128,1]{2,1,3,0:T(1,128)S(1)} fusion(f32[8,16,128,128]{2,3,1,0:T(8,128)} %copy-done, f32[8,16,128,1]{2,3,1,0:T(1,128)S(1)} %bitcast.130), kind=kOutput, calls=%fused_computation.50 | convolution fusion | flops 25165824 | bytes 8458240 | tf_op jit(solution)/shard_map/skij,skj->si/dot_general | solution.py:53
  374.8 9.4 %fusion.24 = f32[8,1,16,128]{3,1,2,0:T(1,128)S(1)} fusion(f32[8,16,128,128]{2,3,1,0:T(8,128)} %copy-done, f32[8,128,1,1]{1,2,3,0:T(1,128)S(1)} %bitcast.142), kind=kOutput, calls=%fused_computation.51 | convolution fusion | flops 25165824 | bytes 8458240 | tf_op jit(solution)/shard_map/skij,si->skj/dot_general | solution.py:55
  384.3 0.8 fusion.7
  385.1 0.0 all-reduce.12.cloned.1.call-update
  385.1 83.3 %all-reduce.12.cloned.1.call-done = f32[128,128]{1,0:T(8,128)} async-done(((f32[128,128]{1,0:T(8,128)}), f32[128,128]{1,0:T(8,128)}) %all-reduce.12.cloned.1.call-update) | async-done | bytes 65552
  468.4 1.4 multiply_reduce_fusion.2
  469.8 32.4 %psum.39 = f32[]{:T(128)} all-reduce(f32[]{:T(128)} %multiply_reduce_fusion.2), channel_id=1, replica_groups=mesh['pairs'=2,'src'=16] {'src'}, use_global_device_ids=true, to_apply=%region_14.15 | all-reduce | flops 1 | bytes 8 | tf_op jit(solution)/shard_map/psum | solution.py:62
  502.9 1.4 multiply_bitcast_fusion
  (4 shorter events, 0.0 us)
Async XLA Ops:
  7.2 30.8 %copy-start.2 = (bf16[1024,256]{1,0:T(8,128)(2,1)S(1)}, bf16[1024,256]{1,0:T(8,128)(2,1)}, u32[]{:S(2)}) copy-start(bf16[1024,256]{1,0:T(8,128)(2,1)} %param.9) | copy-start | bytes 1572868
  7.2 31.0 %copy-start.6 = (s32[8]{0:T(128)S(1)}, s32[8]{0:T(128)}, u32[]{:S(2)}) copy-start(s32[8]{0:T(128)} %param.12) | copy-start | bytes 100
  7.2 31.1 %copy-start.5 = (s32[8]{0:T(128)S(1)}, s32[8]{0:T(128)}, u32[]{:S(2)}) copy-start(s32[8]{0:T(128)} %param.17) | copy-start | bytes 100
  7.2 50.2 %copy-start.7 = (f32[1024]{0:T(1024)S(1)}, f32[1024]{0:T(1024)}, u32[]{:S(2)}) copy-start(f32[1024]{0:T(1024)} %param.13) | copy-start | bytes 12292
  7.2 153.7 %all-reduce.8.cloned.1.call-start = ((), (), s32[]{:S(2)}) async-start(), calls=%async_computation | async-start | bytes 131072
  65.3 11.8 %copy-start = (f32[8,16,128,128]{2,3,1,0:T(8,128)}, f32[8,16,128,128]{2,3,1,0:T(8,128)S(1)}, u32[]{:S(2)}) copy-start(f32[8,16,128,128]{2,3,1,0:T(8,128)S(1)} %fusion.6) | copy-start | bytes 25165828
  65.3 4.6 copy-start.4
  65.4 12.6 %copy-start.3 = (f32[1024]{0:T(1024)S(1)}, f32[1024]{0:T(1024)}, u32[]{:S(2)}) copy-start(f32[1024]{0:T(1024)} %param.16) | copy-start | bytes 12292
  65.4 13.9 %copy-start.8 = (u32[32]{0:T(128)S(1)}, u32[32]{0:T(128)}, u32[]{:S(2)}) copy-start(u32[32]{0:T(128)} %constant.30) | copy-start | bytes 388
  77.9 236.6 %all-reduce.10.cloned.1.call-start = ((), (), s32[]{:S(2)}) async-start(), calls=%async_computation.1 | async-start | bytes 131072
  215.6 7.7 %copy-start.1 = (f32[8,16,128,128]{2,3,1,0:T(8,128)S(1)}, f32[8,16,128,128]{2,3,1,0:T(8,128)}, u32[]{:S(2)}) copy-start(f32[8,16,128,128]{2,3,1,0:T(8,128)} %copy-done) | copy-start | bytes 25165828
  231.2 237.2 %all-reduce.12.cloned.1.call-start = ((), (), s32[]{:S(2)}) async-start(), calls=%async_computation.2 | async-start | bytes 131072
Sparse Core Ops, SparseCore 0:
  78.0 82.8 all-reduce.7
  231.3 83.1 all-reduce.9
  385.2 83.1 all-reduce.11
where the time goes:
time: 511 us
  waiting for transfers between devices  247 us (48%)
  blocking collectives  173 us (34%)
  matrix products  53 us (10%)
  between operations  18 us (4%)
  other arithmetic  15 us (3%)
    unnamed x6, waiting for transfers between devices  247 us
    psum x2, blocking collectives, shards(): mass = lax.psum(jnp.sum(tgt_own * col_sums), 'src')  64.7 us
    all_gather x3, blocking collectives, shards(): tile_scale = lax.all_gather(tgt_own, 'src', axis=0, tiled=True)[tile_tgt]  52.9 us
    psum x1, blocking collectives, shards(): lax.psum((jnp.sum(amass), jnp.sum(bmass_own)), 'src')  32.4 us
    dot_general x3, matrix products, shards(): jnp.einsum('skij,si->skj', kernel, src_scale, precision=lax.Precision.HIG...  23.6 us
    all_gather x1, blocking collectives, shards(): lax.all_gather(tgt_lin.reshape(local_blocks, block), 'src', axis=0, tiled...  23.5 us
    dot_general x3, matrix products, shards(): jnp.einsum('skij,skj->si', kernel, tile_scale, precision=lax.Precision.HI...  19 us
  transfers between devices with their start and end apart: 3, of which 3 were waited for; matrix products, arithmetic and copies ran while one was open for 0% of the time, Pallas kernels for 0%

commit v1 on v0

v1 whole, which is shorter than its diff:
```python
import functools

import jax
import jax.numpy as jnp
from jax import lax
from jax.experimental import pallas as pl
from jax.experimental.pallas import tpu as pltpu
from jax.sharding import PartitionSpec as P

ITERS = 3
EPS = 0.1
RHO = 1.0
ALPHA = 0.5
F = RHO / (RHO + EPS)

VMEM = pltpu.VMEM
SMEM = pltpu.SMEM
ANY = pl.ANY


def diag_mask(block):
    return lax.broadcasted_iota(jnp.int32, (block, block), 0) == lax.broadcasted_iota(
        jnp.int32, (block, block), 1
    )


def to_column(row, mask):
    return jnp.sum(jnp.where(mask, row, 0.0), axis=1, keepdims=True)


def to_row(column, mask):
    return jnp.sum(jnp.where(mask, column, 0.0), axis=0, keepdims=True)


def build_kernel(live, x_ref, feat, lin_ref, mass_ref, k_ref, la_ref, ybuf, sems):
    blocks, slots, block, width = ybuf.shape

    def copy(s):
        return pltpu.make_async_copy(feat.at[s], ybuf.at[s], sems.at[s])

    for s in range(blocks):
        copy(s).start()
    mask = diag_mask(block)
    ones = jnp.ones((8, width), jnp.bfloat16)
    nt = (((1,), (1,)), ((), ()))
    for s in range(blocks):
        x = x_ref[s * block : (s + 1) * block, :]
        x32 = x.astype(jnp.float32)
        sq = jnp.sum(x32 * x32, axis=1, keepdims=True)
        lin = to_column(lin_ref[s : s + 1, :], mask)
        base = (2.0 - sq / width - ALPHA * lin) / EPS
        la = F * jnp.log(to_column(mass_ref[s : s + 1, :], mask))
        la_ref[s * block : (s + 1) * block, :] = jnp.broadcast_to(la, (block, block))
        copy(s).wait()

        def tile(k, _):
            y = ybuf[s, k]
            y32 = y.astype(jnp.float32)
            y2 = y32 * y32
            hi = y2.astype(jnp.bfloat16)
            lo = (y2 - hi.astype(jnp.float32)).astype(jnp.bfloat16)
            cross = lax.dot_general(x, y, nt, preferred_element_type=jnp.float32)
            ysq = lax.dot_general(ones, hi, nt, preferred_element_type=jnp.float32)
            ysq += lax.dot_general(ones, lo, nt, preferred_element_type=jnp.float32)
            e = base + (2.0 / (width * EPS)) * cross - ysq[0:1, :] / (width * EPS)
            start = pl.multiple_of((s * slots + k) * block, block)
            k_ref[pl.ds(start, block), :] = jnp.exp(e)
            return 0

        lax.fori_loop(0, live[s], tile, 0)


def power_of_ratio(num, den):
    return jnp.exp(F * (jnp.log(num) - jnp.log(den)))


def sweep(live, tgt, idx_ref, w_ref, k_ref, la_ref, dense_ref, acc_ref, u_ref, col_ref):
    blocks, slots = tgt.shape
    block = w_ref.shape[1]
    for s in range(blocks):

        def add_row(k, acc):
            w = w_ref[pl.ds(tgt[s, k], 1), :]
            start = pl.multiple_of((s * slots + k) * block, block)
            return acc + k_ref[pl.ds(start, block), :] * w

        acc_ref[s * block : (s + 1) * block, :] = lax.fori_loop(
            0, live[s], add_row, jnp.zeros((block, block), jnp.float32)
        )
    for s in range(blocks):
        rows = pl.ds(s * block, block)
        total = jnp.sum(acc_ref[rows, :], axis=1, keepdims=True)
        u_ref[rows, :] = jnp.exp(la_ref[rows, :] - F * jnp.log(total))
    col_ref[...] = jnp.zeros_like(col_ref)
    for s in range(blocks):
        u = u_ref[s * block : (s + 1) * block, :]

        def add_col(k, _):
            start = pl.multiple_of((s * slots + k) * block, block)
            col_ref[pl.ds(s * slots + k, 1), :] = jnp.sum(
                k_ref[pl.ds(start, block), :] * u, axis=0, keepdims=True
            )
            return 0

        lax.fori_loop(0, live[s], add_col, 0)
    col = col_ref[...]
    hit = lax.broadcasted_iota(jnp.int32, (dense_ref.shape[0], blocks * slots), 0) == idx_ref[...]
    hit = jnp.where(hit, 1.0, 0.0).astype(jnp.bfloat16)
    dense = jnp.zeros(dense_ref.shape, jnp.float32)
    for _ in range(3):
        piece = col.astype(jnp.bfloat16)
        dense += jnp.dot(hit, piece, preferred_element_type=jnp.float32)
        col = col - piece.astype(jnp.float32)
    dense_ref[...] = dense


def total_of(x):
    return jnp.sum(jnp.sum(x, axis=0, keepdims=True), axis=1, keepdims=True)


def first_sweep(n, live, tgt, me, idx_ref, *refs):
    parts = refs[:n]
    k_ref, la_ref, dense_ref, b_ref, et_ref, tot_ref, w_ref, acc_ref, u_ref, col_ref = refs[n:]
    local = parts[0].shape[0] // 3
    for d in range(n):
        rows = pl.ds(pl.multiple_of((me[0] ^ d) * local, local), local)
        b = parts[d][0:local, :]
        et = jnp.exp((-ALPHA / EPS) * parts[d][local : 2 * local, :])
        b_ref[rows, :] = b
        et_ref[rows, :] = et
        w_ref[rows, :] = jnp.where(b > 0.0, et, 0.0)
    am = sum(total_of(parts[d][2 * local : 3 * local, :]) for d in range(n))
    tot = jnp.sqrt(am * total_of(b_ref[...]))
    tot_ref[...] = jnp.broadcast_to(tot, tot_ref.shape)
    sweep(live, tgt, idx_ref, w_ref, k_ref, la_ref, dense_ref, acc_ref, u_ref, col_ref)


def new_scale(mine, other, b_ref, et_ref, tot_ref):
    et = et_ref[...]
    b = b_ref[...]
    col = (mine[...] + other[...]) * et
    t = jnp.where(b > 0.0, power_of_ratio(b, col), 0.0)
    factor = jnp.sqrt(tot_ref[0:1, 0:1] / total_of(t * col))
    return t, factor


def next_sweep(
    live, tgt, idx_ref, mine, other, b_ref, et_ref, tot_ref, k_ref, la_ref,
    dense_ref, u_ref, w_ref, acc_ref, col_ref,
):
    t, factor = new_scale(mine, other, b_ref, et_ref, tot_ref)
    w_ref[...] = t * factor * et_ref[...]
    sweep(live, tgt, idx_ref, w_ref, k_ref, la_ref, dense_ref, acc_ref, u_ref, col_ref)


def last_kernel(me, mine, other, b_ref, et_ref, tot_ref, u_ref, src_ref, tgt_ref, t_ref):
    local, block = src_ref.shape
    t, factor = new_scale(mine, other, b_ref, et_ref, tot_ref)
    t_ref[...] = t * factor
    tgt_ref[...] = t_ref[pl.ds(pl.multiple_of(me[0] * local, local), local), :]
    mask = diag_mask(block)
    for s in range(local):
        src_ref[s : s + 1, :] = to_row(u_ref[s * block : (s + 1) * block, :] * factor, mask)


def call(kernel, ins, outs, scratch=(), smem=0, anys=(), vmem_mb=32, **cost):
    specs = [pl.BlockSpec(memory_space=SMEM)] * smem
    for at in range(smem, len(ins)):
        specs.append(pl.BlockSpec(memory_space=ANY if at in anys else VMEM))
    return pl.pallas_call(
        kernel,
        out_shape=outs,
        in_specs=specs,
        out_specs=[pl.BlockSpec(memory_space=VMEM)] * len(outs),
        scratch_shapes=scratch,
        compiler_params=pltpu.CompilerParams(vmem_limit_bytes=vmem_mb << 20),
        cost_estimate=pl.CostEstimate(**cost) if cost else None,
    )(*ins)


def exchange(x, n, d):
    return lax.ppermute(x, "src", [(i, i ^ d) for i in range(n)])


def shards(
    src_feat, tile_feat, tile_tgt, tile_live, src_lin, tgt_lin, src_mass, tgt_mass, tgt_count
):
    f32 = jnp.float32
    local, slots, block, width = tile_feat.shape
    n = lax.axis_size("src")
    me = lax.axis_index("src").astype(jnp.int32).reshape(1)
    every = local * n
    pairs = local * slots
    valid = lax.broadcasted_iota(jnp.int32, (local, block), 1) < tgt_count[:, None]
    bmass = jnp.where(valid, tgt_mass.reshape(local, block), 0.0)
    amass = src_mass.reshape(local, block)
    own = jnp.concatenate([bmass, tgt_lin.reshape(local, block), amass], axis=0)
    parts = [own] + [exchange(own, n, d) for d in range(1, n)]
    grid = jax.ShapeDtypeStruct((pairs * block, block), f32)
    tall = jax.ShapeDtypeStruct((local * block, block), f32)
    wide = jax.ShapeDtypeStruct((every, block), f32)
    one = jax.ShapeDtypeStruct((8, block), f32)
    kern, la = call(
        build_kernel,
        (tile_live, src_feat, tile_feat, src_lin.reshape(local, block), amass),
        (grid, tall),
        scratch=[VMEM(tile_feat.shape, tile_feat.dtype), pltpu.SemaphoreType.DMA((local,))],
        smem=1,
        anys=(2,),
        flops=2 * pairs * block * block * width,
        bytes_accessed=2 * pairs * block * width,
        transcendentals=pairs * block * block,
    )
    idx = tile_tgt.reshape(1, pairs)
    work = [VMEM((local * block, block), f32), VMEM((pairs, block), f32)]
    w_work = VMEM((every, block), f32)
    dense, b_all, et_all, tot = call(
        functools.partial(first_sweep, n),
        (tile_live, tile_tgt, me, idx, *parts, kern, la),
        (wide, wide, wide, one),
        scratch=[w_work, work[0], VMEM((local * block, block), f32), work[1]],
        smem=3,
    )
    u = None
    for iteration in range(ITERS):
        d = 1
        while d < n:
            other = exchange(dense, n, d)
            if 2 * d < n:
                dense = dense + other
            d *= 2
        if iteration < ITERS - 1:
            dense, u = call(
                next_sweep,
                (tile_live, tile_tgt, idx, dense, other, b_all, et_all, tot, kern, la),
                (wide, tall),
                scratch=[w_work, *work],
                smem=2,
            )
    out = jax.ShapeDtypeStruct((local, block), f32)
    src, tgt = call(
        last_kernel,
        (me, dense, other, b_all, et_all, tot, u),
        (out, out),
        scratch=[w_work],
        smem=1,
    )
    return (src.reshape(-1), tgt.reshape(-1))


def solution(mesh):
    split = P(("pairs", "src"))
    rows = P(("pairs", "src"), None)
    in_specs = (rows, P(("pairs", "src"), None, None, None), rows) + (split,) * 6
    return jax.shard_map(
        shards, mesh=mesh, in_specs=in_specs, out_specs=(split, split), check_vma=False
    )
```

time: 511 us -> 126 us (0.25)
  waiting for transfers between devices: 247 us -> 39.7 us
  blocking collectives: 173 us -> 0 us
  matrix products: 53 us -> 0 us
  starting transfers between devices: 0.12 us -> 51.1 us
  Pallas kernels: 0 us -> 21.4 us
  between operations: 18 us -> 0.84 us
  other arithmetic: 15 us -> 1.56 us
  local copies, waits for them, and re-layouts: 4.1 us -> 13.2 us
    unnamed x6 -> x0, waiting for transfers between devices: 247 us -> none
    psum x3 -> x0, blocking collectives: 97.1 us -> none  [the longest x2 64.7 us: shards(): mass = lax.psum(jnp.sum(tgt_own * col_sums), 'src')]
    all_gather x4 -> x0, blocking collectives: 76.4 us -> none  [the longest x3 52.9 us: shards(): tile_scale = lax.all_gather(tgt_own, 'src', axis=0, tiled=True)[tile_tgt]]
    dot_general x10 -> x0, matrix products: 53 us -> none  [the longest x3 23.6 us: shards(): jnp.einsum('skij,si->skj', kernel, src_scale, precision=lax.Precision.HIG...]
    ppermute x0 -> x27, starting transfers between devices: none -> 51.1 us  [exchange(): return lax.ppermute(x, 'src', [(i, i ^ d) for i in range(n)])]
    ppermute x0 -> x27, waiting for transfers between devices: none -> 39.7 us  [exchange(): return lax.ppermute(x, 'src', [(i, i ^ d) for i in range(n)])]
    pallas_call x0 -> x5, Pallas kernels: none -> 21.4 us  [call(): pl.pallas_call(kernel, out_shape=outs, in_specs=specs, out_specs=[pl.Bloc...]
    unnamed x19 -> x18, local copies, waits for them, and re-layouts: 0.69 us -> 13.1 us
  transfers between devices with their start and end apart: 3 -> 27, of which waited for: 3 -> 13; matrix products, arithmetic and copies ran while one was open for 0% -> 0% of each run, Pallas kernels for 0% -> 9%
where the time goes in v1:
time: 126 us; the launch traced here: 128 us
  starting transfers between devices  51.1 us (41%)
  waiting for transfers between devices  39.7 us (32%)
  Pallas kernels  21.4 us (17%)
  local copies, waits for them, and re-layouts  13.2 us (10%)
  other arithmetic  1.56 us (1%)
    ppermute x27, starting transfers between devices, exchange(): return lax.ppermute(x, 'src', [(i, i ^ d) for i in range(n)])  51.1 us
    ppermute x27, waiting for transfers between devices, exchange(): return lax.ppermute(x, 'src', [(i, i ^ d) for i in range(n)])  39.7 us
    pallas_call x5, Pallas kernels, call(): pl.pallas_call(kernel, out_shape=outs, in_specs=specs, out_specs=[pl.Bloc...  21.4 us
    unnamed x18, local copies, waits for them, and re-layouts  13.1 us
  transfers between devices with their start and end apart: 27, of which 13 were waited for; matrix products, arithmetic and copies ran while one was open for 0% of the time, Pallas kernels for 9%

profile of v1, /device:TPU:0, one launch (start us, length us, event | category | flops | bytes accessed | tf_op | source)
XLA Modules:
  0.0 127.7 jit_solution(15668946704707127248)
XLA Ops:
  0.6 0.0 copy-start.7
  0.7 0.8 bitcast_select_fusion
  1.4 0.7 pad_maximum_fusion.refs_0_
  2.1 5.4 %collective-permute-start.14 = (f32[24,128]{1,0:T(8,128)S(1)}, f32[24,128]{1,0:T(8,128)S(1)}, u32[]{:S(2)}, u32[]{:S(2)}) collective-permute-start(f32[24,128]{1,0:T(8,128)S(1)} %pad_maximum_fusion.refs_0_), channel_id=1, source_target_pairs={{0,15},{1,14},{2,13},{3,12},{4,11},{5,10},{6,9},{7,8},{8,7},{9,6},... | collective-permute-start | bytes 36872 | tf_op jit(solution)/shard_map/ppermute | solution.py:182
  7.6 0.6 collective-permute-start.13
  8.2 3.2 %collective-permute-start.12 = (f32[24,128]{1,0:T(8,128)S(1)}, f32[24,128]{1,0:T(8,128)S(1)}, u32[]{:S(2)}, u32[]{:S(2)}) collective-permute-start(f32[24,128]{1,0:T(8,128)S(1)} %pad_maximum_fusion.refs_0_), channel_id=1, source_target_pairs={{0,13},{1,12},{2,15},{3,14},{4,9},{5,8},{6,11},{7,10},{8,5},{9,4},... | collective-permute-start | bytes 36872 | tf_op jit(solution)/shard_map/ppermute | solution.py:182
  11.4 0.3 collective-permute-start.11
  11.7 0.0 collective-permute-start.10
  11.7 0.0 collective-permute-done.14.refs_15_
  11.7 3.6 %collective-permute-start.9 = (f32[24,128]{1,0:T(8,128)S(1)}, f32[24,128]{1,0:T(8,128)S(1)}, u32[]{:S(2)}, u32[]{:S(2)}) collective-permute-start(f32[24,128]{1,0:T(8,128)S(1)} %pad_maximum_fusion.refs_0_), channel_id=1, source_target_pairs={{0,10},{1,11},{2,8},{3,9},{4,14},{5,15},{6,12},{7,13},{8,2},{9,3},... | collective-permute-start | bytes 36872 | tf_op jit(solution)/shard_map/ppermute | solution.py:182
  15.3 0.0 collective-permute-done.13.refs_14_
  15.3 0.0 collective-permute-start.8
  15.3 0.0 collective-permute-done.12.refs_13_
  15.3 2.6 %collective-permute-start.7 = (f32[24,128]{1,0:T(8,128)S(1)}, f32[24,128]{1,0:T(8,128)S(1)}, u32[]{:S(2)}, u32[]{:S(2)}) collective-permute-start(f32[24,128]{1,0:T(8,128)S(1)} %pad_maximum_fusion.refs_0_), channel_id=1, source_target_pairs={{0,8},{1,9},{2,10},{3,11},{4,12},{5,13},{6,14},{7,15},{8,0},{9,1},... | collective-permute-start | bytes 36872 | tf_op jit(solution)/shard_map/ppermute | solution.py:182
  17.9 0.0 collective-permute-done.11.refs_12_
  17.9 1.9 %collective-permute-start.6 = (f32[24,128]{1,0:T(8,128)S(1)}, f32[24,128]{1,0:T(8,128)S(1)}, u32[]{:S(2)}, u32[]{:S(2)}) collective-permute-start(f32[24,128]{1,0:T(8,128)S(1)} %pad_maximum_fusion.refs_0_), channel_id=1, source_target_pairs={{0,7},{1,6},{2,5},{3,4},{4,3},{5,2},{6,1},{7,0},{8,15},{9,14},{10,... | collective-permute-start | bytes 36872 | tf_op jit(solution)/shard_map/ppermute | solution.py:182
  19.8 0.0 collective-permute-done.10.refs_11_
  19.8 0.8 collective-permute-start.5
  20.6 0.0 collective-permute-done.9.refs_10_
  20.6 1.2 collective-permute-start.4
  21.8 0.0 collective-permute-done.8.refs_9_
  21.8 0.5 collective-permute-start.3
  22.3 1.0 collective-permute-start.2
  23.3 0.0 collective-permute-done.6.refs_7_
  23.3 0.8 collective-permute-start.1
  24.1 0.4 collective-permute-done.5.refs_6_
  24.5 3.4 %copy-done.2 = bf16[8,16,128,256]{3,2,1,0:T(8,128)(2,1)S(1)} copy-done((bf16[8,16,128,256]{3,2,1,0:T(8,128)(2,1)S(1)}, bf16[8,16,128,256]{3,2,1,0:T(8,128)(2,1)}, u32[]{:S(2)}) %copy-start.2) | copy-done | bytes 8388632
  27.9 1.0 copy-done.3
  28.9 0.7 copy-done.5
  29.6 0.7 copy-done.6
  30.3 0.7 copy-done.8
  31.0 11.5 %shard_map.104 = (f32[16384,128]{1,0:T(8,128)S(1)}, f32[1024,128]{1,0:T(8,128)S(1)}) custom-call(s32[8]{0:T(128)S(1)} %copy-done.6, bf16[1024,256]{1,0:T(8,128)(2,1)S(1)} %copy-done.3, bf16[8,16,128,256]{3,2,1,0:T(8,128)(2,1)S(1)} %copy-done.2, f32[8,128]{1,0:T(8,128)S(1)} %bitcast.10, f32[8,128]{1,0:T(8,128)S(1)} %bitcast.9), custom_call_target="tpu_custom_call" | custom-call | flops 1073741824 | bytes 8388608 | tf_op jit(solution)/shard_map/pallas_call | solution.py:170
  42.4 3.3 %copy-done = f32[16384,128]{1,0:T(8,128)} copy-done((f32[16384,128]{1,0:T(8,128)}, f32[16384,128]{1,0:T(8,128)S(1)}, u32[]{:S(2)}) %copy-start) | copy-done | bytes 8388632
  45.7 0.1 reshape.30.idx_ref
  45.8 0.0 collective-permute-done.2.refs_3_
  45.8 0.0 collective-permute-done.1.refs_2_
  45.9 3.4 %copy-done.1 = f32[16384,128]{1,0:T(8,128)S(1)} copy-done((f32[16384,128]{1,0:T(8,128)S(1)}, f32[16384,128]{1,0:T(8,128)}, u32[]{:S(2)}) %copy-start.1) | copy-done | bytes 8388632
  49.2 2.8 %shard_map.105 = (f32[128,128]{1,0:T(8,128)S(1)}, f32[128,128]{1,0:T(8,128)S(1)}, f32[128,128]{1,0:T(8,128)S(1)}, f32[8,128]{1,0:T(8,128)S(1)}) custom-call(s32[8]{0:T(128)S(1)} %copy-done.7, s32[8,16]{1,0:T(8,128)S(1)} %copy-done.4, s32[1]{0:T(128)} %bitcast.me, s32[1,128]{1,0:T(1,128)S(1)} %reshape.30.idx_ref, f32[24,128]{1,0:T(8,128)S(1)} %pad_maximum_fusion.refs_0_, ...), custom_call_target="tpu_custom_call" | custom-call | tf_op jit(solution)/shard_map/pallas_call | solution.py:170
  52.0 9.9 %collective-permute-start.15 = (f32[128,128]{1,0:T(8,128)S(1)}, f32[128,128]{1,0:T(8,128)S(1)}, u32[]{:S(2)}, u32[]{:S(2)}) collective-permute-start(f32[128,128]{1,0:T(8,128)S(1)} %get-tuple-element.15), channel_id=1, source_target_pairs={{0,1},{1,0},{2,3},{3,2},{4,5},{5,4},{6,7},{7,6},{8,9},{9,8},{10,11... | collective-permute-start | bytes 196616 | tf_op jit(solution)/shard_map/ppermute | solution.py:182
  62.0 0.9 collective-permute-done.15
  62.9 9.6 %collective-permute-start.16 = (f32[128,128]{1,0:T(8,128)S(1)}, f32[128,128]{1,0:T(8,128)S(1)}, u32[]{:S(2)}, u32[]{:S(2)}) collective-permute-start(f32[128,128]{1,0:T(8,128)S(1)} %add.27), channel_id=1, source_target_pairs={{0,2},{1,3},{2,0},{3,1},{4,6},{5,7},{6,4},{7,5},{8,10},{9,11},{10,... | collective-permute-start | bytes 196616 | tf_op jit(solution)/shard_map/ppermute | solution.py:182
  72.5 2.4 %collective-permute-done.16 = f32[128,128]{1,0:T(8,128)S(1)} collective-permute-done((f32[128,128]{1,0:T(8,128)S(1)}, f32[128,128]{1,0:T(8,128)S(1)}, u32[]{:S(2)}, u32[]{:S(2)}) %collective-permute-start.16) | collective-permute-done | bytes 65568 | tf_op jit(solution)/shard_map/ppermute | solution.py:182
  74.9 0.1 collective-permute-start.17
  75.0 4.3 %collective-permute-done.17 = f32[128,128]{1,0:T(8,128)S(1)} collective-permute-done((f32[128,128]{1,0:T(8,128)S(1)}, f32[128,128]{1,0:T(8,128)S(1)}, u32[]{:S(2)}, u32[]{:S(2)}) %collective-permute-start.17) | collective-permute-done | bytes 65568 | tf_op jit(solution)/shard_map/ppermute | solution.py:182
  79.3 0.1 collective-permute-start.18
  79.4 5.3 %collective-permute-done.18.other = f32[128,128]{1,0:T(8,128)S(1)} collective-permute-done((f32[128,128]{1,0:T(8,128)S(1)}, f32[128,128]{1,0:T(8,128)S(1)}, u32[]{:S(2)}, u32[]{:S(2)}) %collective-permute-start.18) | collective-permute-done | bytes 65568 | tf_op jit(solution)/shard_map/ppermute | solution.py:182
  84.7 3.4 %shard_map.106 = (f32[128,128]{1,0:T(8,128)S(1)}, f32[1024,128]{1,0:T(8,128)}) custom-call(s32[8]{0:T(128)S(1)} %copy-done.7, s32[8,16]{1,0:T(8,128)S(1)} %copy-done.4, s32[1,128]{1,0:T(1,128)S(1)} %reshape.30.idx_ref, f32[128,128]{1,0:T(8,128)S(1)} %add.29.mine, f32[128,128]{1,0:T(8,128)S(1)} %collective-permute-done.18.other, ...), custom_call_target="tpu_custom_call" | custom-call | tf_op jit(solution)/shard_map/pallas_call | solution.py:170
  88.1 1.3 collective-permute-done.19
  89.4 4.5 %collective-permute-start.20 = (f32[128,128]{1,0:T(8,128)S(1)}, f32[128,128]{1,0:T(8,128)S(1)}, u32[]{:S(2)}, u32[]{:S(2)}) collective-permute-start(f32[128,128]{1,0:T(8,128)S(1)} %add.30), channel_id=1, source_target_pairs={{0,2},{1,3},{2,0},{3,1},{4,6},{5,7},{6,4},{7,5},{8,10},{9,11},{10,... | collective-permute-start | bytes 196616 | tf_op jit(solution)/shard_map/ppermute | solution.py:182
  93.9 2.4 %collective-permute-done.20 = f32[128,128]{1,0:T(8,128)S(1)} collective-permute-done((f32[128,128]{1,0:T(8,128)S(1)}, f32[128,128]{1,0:T(8,128)S(1)}, u32[]{:S(2)}, u32[]{:S(2)}) %collective-permute-start.20) | collective-permute-done | bytes 65568 | tf_op jit(solution)/shard_map/ppermute | solution.py:182
  96.3 0.1 collective-permute-start.21
  96.4 4.3 %collective-permute-done.21 = f32[128,128]{1,0:T(8,128)S(1)} collective-permute-done((f32[128,128]{1,0:T(8,128)S(1)}, f32[128,128]{1,0:T(8,128)S(1)}, u32[]{:S(2)}, u32[]{:S(2)}) %collective-permute-start.21) | collective-permute-done | bytes 65568 | tf_op jit(solution)/shard_map/ppermute | solution.py:182
  100.7 0.1 collective-permute-start.22
  100.7 5.3 %collective-permute-done.22.other = f32[128,128]{1,0:T(8,128)S(1)} collective-permute-done((f32[128,128]{1,0:T(8,128)S(1)}, f32[128,128]{1,0:T(8,128)S(1)}, u32[]{:S(2)}, u32[]{:S(2)}) %collective-permute-start.22) | collective-permute-done | bytes 65568 | tf_op jit(solution)/shard_map/ppermute | solution.py:182
  106.0 2.8 %shard_map.107 = (f32[128,128]{1,0:T(8,128)S(1)}, f32[1024,128]{1,0:T(8,128)S(1)}) custom-call(s32[8]{0:T(128)S(1)} %copy-done.7, s32[8,16]{1,0:T(8,128)S(1)} %copy-done.4, s32[1,128]{1,0:T(1,128)S(1)} %reshape.30.idx_ref, f32[128,128]{1,0:T(8,128)S(1)} %add.32.mine, f32[128,128]{1,0:T(8,128)S(1)} %collective-permute-done.22.other, ...), custom_call_target="tpu_custom_call" | custom-call | tf_op jit(solution)/shard_map/pallas_call | solution.py:170
  108.9 0.1 collective-permute-start.23
  108.9 1.2 collective-permute-done.23
  110.2 4.5 %collective-permute-start.24 = (f32[128,128]{1,0:T(8,128)S(1)}, f32[128,128]{1,0:T(8,128)S(1)}, u32[]{:S(2)}, u32[]{:S(2)}) collective-permute-start(f32[128,128]{1,0:T(8,128)S(1)} %add.33), channel_id=1, source_target_pairs={{0,2},{1,3},{2,0},{3,1},{4,6},{5,7},{6,4},{7,5},{8,10},{9,11},{10,... | collective-permute-start | bytes 196616 | tf_op jit(solution)/shard_map/ppermute | solution.py:182
  114.7 2.4 %collective-permute-done.24 = f32[128,128]{1,0:T(8,128)S(1)} collective-permute-done((f32[128,128]{1,0:T(8,128)S(1)}, f32[128,128]{1,0:T(8,128)S(1)}, u32[]{:S(2)}, u32[]{:S(2)}) %collective-permute-start.24) | collective-permute-done | bytes 65568 | tf_op jit(solution)/shard_map/ppermute | solution.py:182
  117.2 0.1 collective-permute-start.25
  117.2 4.3 %collective-permute-done.25 = f32[128,128]{1,0:T(8,128)S(1)} collective-permute-done((f32[128,128]{1,0:T(8,128)S(1)}, f32[128,128]{1,0:T(8,128)S(1)}, u32[]{:S(2)}, u32[]{:S(2)}) %collective-permute-start.25) | collective-permute-done | bytes 65568 | tf_op jit(solution)/shard_map/ppermute | solution.py:182
  121.5 0.1 collective-permute-start.26
  121.6 5.3 %collective-permute-done.26.other = f32[128,128]{1,0:T(8,128)S(1)} collective-permute-done((f32[128,128]{1,0:T(8,128)S(1)}, f32[128,128]{1,0:T(8,128)S(1)}, u32[]{:S(2)}, u32[]{:S(2)}) %collective-permute-start.26) | collective-permute-done | bytes 65568 | tf_op jit(solution)/shard_map/ppermute | solution.py:182
  126.9 0.8 shard_map.108
  (25 shorter events, 0.1 us)
Async XLA Ops:
  0.6 45.2 %copy-start.7 = (s32[8]{0:T(128)S(1)}, s32[8]{0:T(128)}, u32[]{:S(2)}) copy-start(s32[8]{0:T(128)} %live.7) | copy-start | bytes 100
  0.6 45.1 %copy-start.4 = (s32[8,16]{1,0:T(8,128)S(1)}, s32[8,16]{1,0:T(8,128)}, u32[]{:S(2)}) copy-start(s32[8,16]{1,0:T(8,128)} %tgt.5) | copy-start | bytes 1540
  2.1 9.6 %collective-permute-start.14 = (f32[24,128]{1,0:T(8,128)S(1)}, f32[24,128]{1,0:T(8,128)S(1)}, u32[]{:S(2)}, u32[]{:S(2)}) collective-permute-start(f32[24,128]{1,0:T(8,128)S(1)} %pad_maximum_fusion.refs_0_), channel_id=1, source_target_pairs={{0,15},{1,14},{2,13},{3,12},{4,11},{5,10},{6,9},{7,8},{8,7},{9,6},... | collective-permute-start | bytes 36872 | tf_op jit(solution)/shard_map/ppermute | solution.py:182
  7.6 7.7 %collective-permute-start.13 = (f32[24,128]{1,0:T(8,128)S(1)}, f32[24,128]{1,0:T(8,128)S(1)}, u32[]{:S(2)}, u32[]{:S(2)}) collective-permute-start(f32[24,128]{1,0:T(8,128)S(1)} %pad_maximum_fusion.refs_0_), channel_id=1, source_target_pairs={{0,14},{1,15},{2,12},{3,13},{4,10},{5,11},{6,8},{7,9},{8,6},{9,7},... | collective-permute-start | bytes 36872 | tf_op jit(solution)/shard_map/ppermute | solution.py:182
  8.2 7.1 %collective-permute-start.12 = (f32[24,128]{1,0:T(8,128)S(1)}, f32[24,128]{1,0:T(8,128)S(1)}, u32[]{:S(2)}, u32[]{:S(2)}) collective-permute-start(f32[24,128]{1,0:T(8,128)S(1)} %pad_maximum_fusion.refs_0_), channel_id=1, source_target_pairs={{0,13},{1,12},{2,15},{3,14},{4,9},{5,8},{6,11},{7,10},{8,5},{9,4},... | collective-permute-start | bytes 36872 | tf_op jit(solution)/shard_map/ppermute | solution.py:182
  11.4 6.5 %collective-permute-start.11 = (f32[24,128]{1,0:T(8,128)S(1)}, f32[24,128]{1,0:T(8,128)S(1)}, u32[]{:S(2)}, u32[]{:S(2)}) collective-permute-start(f32[24,128]{1,0:T(8,128)S(1)} %pad_maximum_fusion.refs_0_), channel_id=1, source_target_pairs={{0,12},{1,13},{2,14},{3,15},{4,8},{5,9},{6,10},{7,11},{8,4},{9,5},... | collective-permute-start | bytes 36872 | tf_op jit(solution)/shard_map/ppermute | solution.py:182
  11.7 8.1 %collective-permute-start.10 = (f32[24,128]{1,0:T(8,128)S(1)}, f32[24,128]{1,0:T(8,128)S(1)}, u32[]{:S(2)}, u32[]{:S(2)}) collective-permute-start(f32[24,128]{1,0:T(8,128)S(1)} %pad_maximum_fusion.refs_0_), channel_id=1, source_target_pairs={{0,11},{1,10},{2,9},{3,8},{4,15},{5,14},{6,13},{7,12},{8,3},{9,2},... | collective-permute-start | bytes 36872 | tf_op jit(solution)/shard_map/ppermute | solution.py:182
  11.7 8.9 %collective-permute-start.9 = (f32[24,128]{1,0:T(8,128)S(1)}, f32[24,128]{1,0:T(8,128)S(1)}, u32[]{:S(2)}, u32[]{:S(2)}) collective-permute-start(f32[24,128]{1,0:T(8,128)S(1)} %pad_maximum_fusion.refs_0_), channel_id=1, source_target_pairs={{0,10},{1,11},{2,8},{3,9},{4,14},{5,15},{6,12},{7,13},{8,2},{9,3},... | collective-permute-start | bytes 36872 | tf_op jit(solution)/shard_map/ppermute | solution.py:182
  15.3 6.5 %collective-permute-start.8 = (f32[24,128]{1,0:T(8,128)S(1)}, f32[24,128]{1,0:T(8,128)S(1)}, u32[]{:S(2)}, u32[]{:S(2)}) collective-permute-start(f32[24,128]{1,0:T(8,128)S(1)} %pad_maximum_fusion.refs_0_), channel_id=1, source_target_pairs={{0,9},{1,8},{2,11},{3,10},{4,13},{5,12},{6,15},{7,14},{8,1},{9,0},... | collective-permute-start | bytes 36872 | tf_op jit(solution)/shard_map/ppermute | solution.py:182
  15.3 7.0 %collective-permute-start.7 = (f32[24,128]{1,0:T(8,128)S(1)}, f32[24,128]{1,0:T(8,128)S(1)}, u32[]{:S(2)}, u32[]{:S(2)}) collective-permute-start(f32[24,128]{1,0:T(8,128)S(1)} %pad_maximum_fusion.refs_0_), channel_id=1, source_target_pairs={{0,8},{1,9},{2,10},{3,11},{4,12},{5,13},{6,14},{7,15},{8,0},{9,1},... | collective-permute-start | bytes 36872 | tf_op jit(solution)/shard_map/ppermute | solution.py:182
  17.9 5.4 %collective-permute-start.6 = (f32[24,128]{1,0:T(8,128)S(1)}, f32[24,128]{1,0:T(8,128)S(1)}, u32[]{:S(2)}, u32[]{:S(2)}) collective-permute-start(f32[24,128]{1,0:T(8,128)S(1)} %pad_maximum_fusion.refs_0_), channel_id=1, source_target_pairs={{0,7},{1,6},{2,5},{3,4},{4,3},{5,2},{6,1},{7,0},{8,15},{9,14},{10,... | collective-permute-start | bytes 36872 | tf_op jit(solution)/shard_map/ppermute | solution.py:182
  19.8 4.7 %collective-permute-start.5 = (f32[24,128]{1,0:T(8,128)S(1)}, f32[24,128]{1,0:T(8,128)S(1)}, u32[]{:S(2)}, u32[]{:S(2)}) collective-permute-start(f32[24,128]{1,0:T(8,128)S(1)} %pad_maximum_fusion.refs_0_), channel_id=1, source_target_pairs={{0,6},{1,7},{2,4},{3,5},{4,2},{5,3},{6,0},{7,1},{8,14},{9,15},{10,... | collective-permute-start | bytes 36872 | tf_op jit(solution)/shard_map/ppermute | solution.py:182
  20.6 25.2 %collective-permute-start.4 = (f32[24,128]{1,0:T(8,128)S(1)}, f32[24,128]{1,0:T(8,128)S(1)}, u32[]{:S(2)}, u32[]{:S(2)}) collective-permute-start(f32[24,128]{1,0:T(8,128)S(1)} %pad_maximum_fusion.refs_0_), channel_id=1, source_target_pairs={{0,5},{1,4},{2,7},{3,6},{4,1},{5,0},{6,3},{7,2},{8,13},{9,12},{10,... | collective-permute-start | bytes 36872 | tf_op jit(solution)/shard_map/ppermute | solution.py:182
  21.8 24.0 %collective-permute-start.3 = (f32[24,128]{1,0:T(8,128)S(1)}, f32[24,128]{1,0:T(8,128)S(1)}, u32[]{:S(2)}, u32[]{:S(2)}) collective-permute-start(f32[24,128]{1,0:T(8,128)S(1)} %pad_maximum_fusion.refs_0_), channel_id=1, source_target_pairs={{0,4},{1,5},{2,6},{3,7},{4,0},{5,1},{6,2},{7,3},{8,12},{9,13},{10,... | collective-permute-start | bytes 36872 | tf_op jit(solution)/shard_map/ppermute | solution.py:182
  22.3 23.5 %collective-permute-start.2 = (f32[24,128]{1,0:T(8,128)S(1)}, f32[24,128]{1,0:T(8,128)S(1)}, u32[]{:S(2)}, u32[]{:S(2)}) collective-permute-start(f32[24,128]{1,0:T(8,128)S(1)} %pad_maximum_fusion.refs_0_), channel_id=1, source_target_pairs={{0,3},{1,2},{2,1},{3,0},{4,7},{5,6},{6,5},{7,4},{8,11},{9,10},{10,... | collective-permute-start | bytes 36872 | tf_op jit(solution)/shard_map/ppermute | solution.py:182
  23.3 22.5 %collective-permute-start.1 = (f32[24,128]{1,0:T(8,128)S(1)}, f32[24,128]{1,0:T(8,128)S(1)}, u32[]{:S(2)}, u32[]{:S(2)}) collective-permute-start(f32[24,128]{1,0:T(8,128)S(1)} %pad_maximum_fusion.refs_0_), channel_id=1, source_target_pairs={{0,2},{1,3},{2,0},{3,1},{4,6},{5,7},{6,4},{7,5},{8,10},{9,11},{10,... | collective-permute-start | bytes 36872 | tf_op jit(solution)/shard_map/ppermute | solution.py:182
  24.5 21.3 %collective-permute-start = (f32[24,128]{1,0:T(8,128)S(1)}, f32[24,128]{1,0:T(8,128)S(1)}, u32[]{:S(2)}, u32[]{:S(2)}) collective-permute-start(f32[24,128]{1,0:T(8,128)S(1)} %pad_maximum_fusion.refs_0_), channel_id=1, source_target_pairs={{0,1},{1,0},{2,3},{3,2},{4,5},{5,4},{6,7},{7,6},{8,9},{9,8},{10,11... | collective-permute-start | bytes 36872 | tf_op jit(solution)/shard_map/ppermute | solution.py:182
  24.5 3.4 %copy-start.2 = (bf16[8,16,128,256]{3,2,1,0:T(8,128)(2,1)S(1)}, bf16[8,16,128,256]{3,2,1,0:T(8,128)(2,1)}, u32[]{:S(2)}) copy-start(bf16[8,16,128,256]{3,2,1,0:T(8,128)(2,1)} %feat.1) | copy-start | bytes 25165828
  27.9 1.0 copy-start.3
  28.9 0.7 copy-start.5
  29.6 0.7 copy-start.6
  30.3 0.7 copy-start.8
  42.4 3.3 %copy-start = (f32[16384,128]{1,0:T(8,128)}, f32[16384,128]{1,0:T(8,128)S(1)}, u32[]{:S(2)}) copy-start(f32[16384,128]{1,0:T(8,128)S(1)} %get-tuple-element.13.refs_16_.k_ref) | copy-start | bytes 25165828
  45.8 3.4 %copy-start.1 = (f32[16384,128]{1,0:T(8,128)S(1)}, f32[16384,128]{1,0:T(8,128)}, u32[]{:S(2)}) copy-start(f32[16384,128]{1,0:T(8,128)} %copy-done) | copy-start | bytes 25165828
  52.0 10.8 %collective-permute-start.15 = (f32[128,128]{1,0:T(8,128)S(1)}, f32[128,128]{1,0:T(8,128)S(1)}, u32[]{:S(2)}, u32[]{:S(2)}) collective-permute-start(f32[128,128]{1,0:T(8,128)S(1)} %get-tuple-element.15), channel_id=1, source_target_pairs={{0,1},{1,0},{2,3},{3,2},{4,5},{5,4},{6,7},{7,6},{8,9},{9,8},{10,11... | collective-permute-start | bytes 196616 | tf_op jit(solution)/shard_map/ppermute | solution.py:182
  62.9 12.0 %collective-permute-start.16 = (f32[128,128]{1,0:T(8,128)S(1)}, f32[128,128]{1,0:T(8,128)S(1)}, u32[]{:S(2)}, u32[]{:S(2)}) collective-permute-start(f32[128,128]{1,0:T(8,128)S(1)} %add.27), channel_id=1, source_target_pairs={{0,2},{1,3},{2,0},{3,1},{4,6},{5,7},{6,4},{7,5},{8,10},{9,11},{10,... | collective-permute-start | bytes 196616 | tf_op jit(solution)/shard_map/ppermute | solution.py:182
  74.9 4.3 %collective-permute-start.17 = (f32[128,128]{1,0:T(8,128)S(1)}, f32[128,128]{1,0:T(8,128)S(1)}, u32[]{:S(2)}, u32[]{:S(2)}) collective-permute-start(f32[128,128]{1,0:T(8,128)S(1)} %add.28), channel_id=1, source_target_pairs={{0,4},{1,5},{2,6},{3,7},{4,0},{5,1},{6,2},{7,3},{8,12},{9,13},{10,... | collective-permute-start | bytes 196616 | tf_op jit(solution)/shard_map/ppermute | solution.py:182
  79.3 5.4 %collective-permute-start.18 = (f32[128,128]{1,0:T(8,128)S(1)}, f32[128,128]{1,0:T(8,128)S(1)}, u32[]{:S(2)}, u32[]{:S(2)}) collective-permute-start(f32[128,128]{1,0:T(8,128)S(1)} %add.29.mine), channel_id=1, source_target_pairs={{0,8},{1,9},{2,10},{3,11},{4,12},{5,13},{6,14},{7,15},{8,0},{9,1},... | collective-permute-start | bytes 196616 | tf_op jit(solution)/shard_map/ppermute | solution.py:182
  88.1 1.3 collective-permute-start.19
  89.4 6.9 %collective-permute-start.20 = (f32[128,128]{1,0:T(8,128)S(1)}, f32[128,128]{1,0:T(8,128)S(1)}, u32[]{:S(2)}, u32[]{:S(2)}) collective-permute-start(f32[128,128]{1,0:T(8,128)S(1)} %add.30), channel_id=1, source_target_pairs={{0,2},{1,3},{2,0},{3,1},{4,6},{5,7},{6,4},{7,5},{8,10},{9,11},{10,... | collective-permute-start | bytes 196616 | tf_op jit(solution)/shard_map/ppermute | solution.py:182
  96.3 4.3 %collective-permute-start.21 = (f32[128,128]{1,0:T(8,128)S(1)}, f32[128,128]{1,0:T(8,128)S(1)}, u32[]{:S(2)}, u32[]{:S(2)}) collective-permute-start(f32[128,128]{1,0:T(8,128)S(1)} %add.31), channel_id=1, source_target_pairs={{0,4},{1,5},{2,6},{3,7},{4,0},{5,1},{6,2},{7,3},{8,12},{9,13},{10,... | collective-permute-start | bytes 196616 | tf_op jit(solution)/shard_map/ppermute | solution.py:182
  100.7 5.4 %collective-permute-start.22 = (f32[128,128]{1,0:T(8,128)S(1)}, f32[128,128]{1,0:T(8,128)S(1)}, u32[]{:S(2)}, u32[]{:S(2)}) collective-permute-start(f32[128,128]{1,0:T(8,128)S(1)} %add.32.mine), channel_id=1, source_target_pairs={{0,8},{1,9},{2,10},{3,11},{4,12},{5,13},{6,14},{7,15},{8,0},{9,1},... | collective-permute-start | bytes 196616 | tf_op jit(solution)/shard_map/ppermute | solution.py:182
  108.9 1.3 %collective-permute-start.23 = (f32[128,128]{1,0:T(8,128)S(1)}, f32[128,128]{1,0:T(8,128)S(1)}, u32[]{:S(2)}, u32[]{:S(2)}) collective-permute-start(f32[128,128]{1,0:T(8,128)S(1)} %get-tuple-element.20), channel_id=1, source_target_pairs={{0,1},{1,0},{2,3},{3,2},{4,5},{5,4},{6,7},{7,6},{8,9},{9,8},{10,11... | collective-permute-start | bytes 196616 | tf_op jit(solution)/shard_map/ppermute | solution.py:182
  110.2 6.9 %collective-permute-start.24 = (f32[128,128]{1,0:T(8,128)S(1)}, f32[128,128]{1,0:T(8,128)S(1)}, u32[]{:S(2)}, u32[]{:S(2)}) collective-permute-start(f32[128,128]{1,0:T(8,128)S(1)} %add.33), channel_id=1, source_target_pairs={{0,2},{1,3},{2,0},{3,1},{4,6},{5,7},{6,4},{7,5},{8,10},{9,11},{10,... | collective-permute-start | bytes 196616 | tf_op jit(solution)/shard_map/ppermute | solution.py:182
  117.2 4.3 %collective-permute-start.25 = (f32[128,128]{1,0:T(8,128)S(1)}, f32[128,128]{1,0:T(8,128)S(1)}, u32[]{:S(2)}, u32[]{:S(2)}) collective-permute-start(f32[128,128]{1,0:T(8,128)S(1)} %add.34), channel_id=1, source_target_pairs={{0,4},{1,5},{2,6},{3,7},{4,0},{5,1},{6,2},{7,3},{8,12},{9,13},{10,... | collective-permute-start | bytes 196616 | tf_op jit(solution)/shard_map/ppermute | solution.py:182
  121.5 5.4 %collective-permute-start.26 = (f32[128,128]{1,0:T(8,128)S(1)}, f32[128,128]{1,0:T(8,128)S(1)}, u32[]{:S(2)}, u32[]{:S(2)}) collective-permute-start(f32[128,128]{1,0:T(8,128)S(1)} %add.35.mine), channel_id=1, source_target_pairs={{0,8},{1,9},{2,10},{3,11},{4,12},{5,13},{6,14},{7,15},{8,0},{9,1},... | collective-permute-start | bytes 196616 | tf_op jit(solution)/shard_map/ppermute | solution.py:182
